TPU v7x, 512 devices: a whole 4x4x16 slice. The times are simulated.
512 devices in a mesh: seq: 16 (over x, y_hi, core), chan: 16 (over z), batch: 2 (over y_lo).
Axes of the slice: x: 4, y: 4 (y_hi: 2, y_lo: 2; y = y_hi * 2 + y_lo), z: 16, core: 2. Of those that a mesh axis runs over, the one named last changes fastest.
Arguments:
- tokens: bfloat16 [8192, 4096], P(('batch', 'seq'), 'chan'), parts along dimension 0, may hold values from -6 to 6
- in_weights: bfloat16 [3, 4096, 4096], P(None, 'seq', 'chan'), may hold values from -0.09375 to 0.09375
- out_weights: bfloat16 [4096, 4096], P('seq', 'chan'), may hold values from -0.09375 to 0.09375
- spectrum: float32 [2, 4096, 8192], P(None, 'chan', 'seq'), may hold values from -6 to 6
Outputs:
- output: bfloat16 [8192, 4096], P(('batch', 'seq'), 'chan'), parts along dimension 0
There are 2 independent parts, one for each index of `batch`. A program takes and returns all parts, laid end to end along the dimension named above; an argument that names none is the same for every part. Nothing has to cross between parts.
All inputs are finite; a program needn't handle non-finite values.
Results may differ from a plain program's by a relative error of at most 0.014.
Values may be sent and summed in bfloat16 or wider, within the bound.
A program may use at most 64 MiB of HBM per device.

v0:
```python
import math

import jax
import jax.numpy as jnp
from jax import lax
from jax.sharding import PartitionSpec as P

highest = lax.Precision.HIGHEST


def joined_along(parts, dim):
    dims = list(parts.shape[1:])
    dims[dim] *= parts.shape[0]
    return jnp.moveaxis(parts, 0, dim).reshape(dims)


def copy_for_each(array, axis):
    devices = lax.axis_size(axis)
    return lax.all_to_all(
        jnp.broadcast_to(array[None], (devices, *array.shape)), axis, 0, 0, tiled=True
    )


def gather_directly(array, axis, dim):
    return joined_along(copy_for_each(array, axis), dim)


def turn_table(first_count, second_count, period, sign_value):
    product = (
        jnp.arange(first_count, dtype=jnp.int32)[:, None]
        * jnp.arange(second_count, dtype=jnp.int32)[None, :]
    )
    turn_angle = (product % period).astype(jnp.float32) * (2.0 * math.pi / period)
    return (jnp.cos(turn_angle), sign_value * jnp.sin(turn_angle))


def times_complex(left_real, left_imag, right_real, right_imag):
    return (
        left_real * right_real - left_imag * right_imag,
        left_real * right_imag + left_imag * right_real,
    )


def table_product(pattern, data_real, data_imag, table_cos, table_sin):
    real_part = jnp.einsum(pattern, data_real, table_cos, precision=highest) - jnp.einsum(
        pattern, data_imag, table_sin, precision=highest
    )
    imag_part = jnp.einsum(pattern, data_real, table_sin, precision=highest) + jnp.einsum(
        pattern, data_imag, table_cos, precision=highest
    )
    return (real_part, imag_part)


def body(tokens, in_weights, out_weights, spectrum):
    seq_count = lax.axis_size("seq")
    features = gather_directly(tokens, "chan", 1)
    tok_rows = features.shape[0]
    padded_len = 2 * seq_count * tok_rows
    twice_seq = 2 * seq_count
    projected = jnp.einsum(
        "prc,mr->pcm",
        lax.all_gather(in_weights, "seq", axis=1, tiled=True),
        features,
        preferred_element_type=jnp.float32,
    )
    outer_gate = projected[0]
    mixed_in = projected[1] * projected[2]
    inner_cos, inner_sin = turn_table(tok_rows, tok_rows, tok_rows, -1.0)
    back_cos, back_sin = turn_table(tok_rows, tok_rows, tok_rows, 1.0)
    spread = lax.all_to_all(spectrum, "seq", split_axis=1, concat_axis=2, tiled=True)
    column = lax.all_to_all(mixed_in, "seq", split_axis=0, concat_axis=1, tiled=True)
    sub_chan = column.shape[0]
    blocks = column.reshape(sub_chan, seq_count, tok_rows)
    first_cos, first_sin = turn_table(twice_seq, seq_count, twice_seq, -1.0)
    a_real = jnp.einsum("ks,csm->ckm", first_cos, blocks, precision=highest)
    a_imag = jnp.einsum("ks,csm->ckm", first_sin, blocks, precision=highest)
    twist_cos, twist_sin = turn_table(twice_seq, tok_rows, padded_len, -1.0)
    b_real, b_imag = times_complex(a_real, a_imag, twist_cos, twist_sin)
    u_real, u_imag = table_product("ckm,mq->ckq", b_real, b_imag, inner_cos, inner_sin)
    shaped = jnp.transpose(spread.reshape(2, sub_chan, tok_rows, twice_seq), (0, 1, 3, 2))
    y_real, y_imag = times_complex(u_real, u_imag, shaped[0], shaped[1])
    c_real, c_imag = table_product("ckq,qm->ckm", y_real, y_imag, back_cos, back_sin)
    untwist_cos, untwist_sin = turn_table(twice_seq, tok_rows, padded_len, 1.0)
    d_real, d_imag = times_complex(c_real, c_imag, untwist_cos, untwist_sin)
    last_cos, last_sin = turn_table(seq_count, twice_seq, twice_seq, 1.0)
    signal = jnp.einsum("sk,ckm->csm", last_cos, d_real, precision=highest) - jnp.einsum(
        "sk,ckm->csm", last_sin, d_imag, precision=highest
    )
    signal = (signal / padded_len).reshape(sub_chan, seq_count * tok_rows)
    convolved = lax.all_to_all(signal, "seq", split_axis=1, concat_axis=0, tiled=True)
    mixed = (outer_gate * convolved).astype(jnp.bfloat16)
    gathered = lax.all_gather(mixed, "chan", axis=0, tiled=True)
    result = lax.dot_general(
        gathered,
        gather_directly(out_weights, "seq", 0),
        (((0,), (0,)), ((), ())),
        preferred_element_type=jnp.float32,
    )
    return result.astype(jnp.bfloat16)


def solution(mesh):
    placed = (
        P(("batch", "seq"), "chan"),
        P(None, "seq", "chan"),
        P("seq", "chan"),
        P(None, "chan", "seq"),
    )
    return jax.shard_map(
        body, mesh=mesh, in_specs=placed, out_specs=P(("batch", "seq"), "chan"), check_vma=False
    )
```

profile of v0, /device:TPU:4, one launch (start us, length us, event | category | flops | bytes accessed | tf_op | source)
XLA Modules:
  0.0 265.8 jit_solution(16160248073597634650)
XLA Ops:
  6.5 0.0 all-gather.3.cloned.1.call-start
  6.5 1.9 copy.13
  8.5 0.0 all-gather.3.cloned.1.call-update
  8.5 2.5 broadcast_in_dim.4
  10.9 0.0 copy-start
  10.9 15.3 %all-to-all-start = ((bf16[16,256,256]{2,1,0:T(8,128)(2,1)}), bf16[16,256,256]{2,1,0:T(8,128)(2,1)S(1)}, u32[]{:S(2)}, u32[]{:S(2)}) async-start(bf16[16,256,256]{2,1,0:T(8,128)(2,1)} %broadcast_in_dim.4), calls=%async_computation | async-start | bytes 4194304 | tf_op jit(solution)/shard_map/all_to_all | solution.py:19
  26.3 0.0 copy-done
  26.3 1.9 copy.16
  28.2 93.7 %all-to-all-done = bf16[16,256,256]{2,1,0:T(8,128)(2,1)S(1)} async-done(((bf16[16,256,256]{2,1,0:T(8,128)(2,1)}), bf16[16,256,256]{2,1,0:T(8,128)(2,1)S(1)}, u32[]{:S(2)}, u32[]{:S(2)}) %all-to-all-start) | async-done | bytes 2097184 | tf_op jit(solution)/shard_map/all_to_all | solution.py:19
  121.9 7.5 %all-to-all-start.2 = ((f32[2,256,512]{2,0,1:T(2,128)}), f32[2,256,512]{2,0,1:T(2,128)S(1)}, u32[]{:S(2)}, u32[]{:S(2)}) async-start(f32[2,256,512]{2,0,1:T(2,128)} %copy.16), calls=%async_computation.2 | async-start | bytes 2097152 | tf_op jit(solution)/shard_map/all_to_all | solution.py:70
  129.3 2.5 copy.14
  131.9 2.9 %reshape.74 = bf16[256,4096,1]{1,0,2:T(8,128)(2,1)S(1)} reshape(bf16[256,16,256]{2,1,0:T(8,128)(2,1)} %copy.14) | data formatting | bytes 4194304 | tf_op jit(solution)/shard_map/reshape | solution.py:14
  134.8 0.0 all-gather.3.cloned.1.call-done
  134.8 4.6 %fusion.136 = f32[3,256,256]{2,1,0:T(8,128)S(1)} fusion(bf16[3,4096,256]{1,2,0:T(8,128)(2,1)} %all-gather.3.cloned.1.call-done, bf16[256,4096,1]{1,0,2:T(8,128)(2,1)S(1)} %reshape.74), kind=kOutput, calls=%fused_computation.154 | convolution fusion | flops 1610612736 | bytes 9175040 | tf_op jit(solution)/shard_map/prc,mr->pcm/dot_general | solution.py:60
  139.4 0.0 copy-start.1
  139.4 0.9 copy-done.1
  140.3 0.8 slice_multiply_fusion
  141.0 4.1 %all-to-all-done.2 = f32[2,256,512]{2,0,1:T(2,128)S(1)} async-done(((f32[2,256,512]{2,0,1:T(2,128)}), f32[2,256,512]{2,0,1:T(2,128)S(1)}, u32[]{:S(2)}, u32[]{:S(2)}) %all-to-all-start.2) | async-done | bytes 1048608 | tf_op jit(solution)/shard_map/all_to_all | solution.py:70
  145.1 5.7 %all-to-all-start.1 = ((f32[16,16,256]{2,1,0:T(8,128)}), f32[16,16,256]{2,1,0:T(8,128)S(1)}, u32[]{:S(2)}, u32[]{:S(2)}) async-start(f32[16,16,256]{2,1,0:T(8,128)} %bitcast.2), calls=%async_computation.1 | async-start | bytes 524288 | tf_op jit(solution)/shard_map/all_to_all | solution.py:71
  150.8 0.0 all-gather.5.cloned.1.call-start
  150.8 0.1 fusion.57
  151.0 0.1 broadcast_multiply_fusion
  151.1 0.6 copy.29
  151.7 2.5 reshape.72
  154.3 3.0 %copy.18 = f32[2,16,256,32]{2,3,1,0:T(8,128)S(1)} copy(f32[2,16,256,32]{3,2,1,0:T(8,128)} %reshape.72) | data formatting | bytes 2097152 | tf_op jit(solution)/shard_map/reshape | solution.py:80
  157.3 0.5 all-to-all-done.1
  157.8 0.7 convolution_bitcast_fusion
  158.5 0.7 convolution_bitcast_fusion.1
  159.2 1.6 fusion.24
  160.8 1.6 fusion.17
  162.4 1.6 convolution_subtract_fusion.1
  164.0 1.6 multiply_add_fusion
  165.6 1.6 fusion.21
  167.2 1.6 fusion.14
  168.7 1.8 convolution_subtract_fusion
  170.5 1.6 convolution_add_fusion
  172.1 0.0 copy-start.2
  172.1 0.5 fusion.5
  172.6 0.5 fusion.1
  173.1 0.2 copy.19
  173.3 13.5 %all_to_all.54 = f32[16,16,256]{2,0,1:T(8,128)S(1)} all-to-all(f32[16,16,256]{2,0,1:T(8,128)S(1)} %copy.19), channel_id=1, replica_groups=mesh['seq'=16,'chan'=16,'batch'=2] {'seq'}, dimensions={1} | all-to-all | bytes 524288 | tf_op jit(solution)/shard_map/all_to_all | solution.py:90
  186.8 1.6 fusion.13
  188.4 0.0 all-gather.5.cloned.1.call-update
  188.4 0.0 copy-done.2
  188.5 0.2 broadcast_in_dim.5
  188.7 31.6 %all_to_all.55 = bf16[16,256,256]{2,1,0:T(8,128)(2,1)S(1)} all-to-all(bf16[16,256,256]{2,1,0:T(8,128)(2,1)S(1)} %broadcast_in_dim.5), channel_id=1, replica_groups=mesh['seq'=16,'chan'=16,'batch'=2] {'seq'}, dimensions={0} | all-to-all | bytes 4194304 | tf_op jit(solution)/shard_map/all_to_all | solution.py:19
  220.2 35.7 %all-gather.5.cloned.1.call-done = bf16[4096,256]{1,0:T(8,128)(2,1)} async-done(((bf16[256,256]{1,0:T(8,128)(2,1)}), bf16[4096,256]{1,0:T(8,128)(2,1)}) %all-gather.5.cloned.1.call-update) | async-done | bytes 2097168 | tf_op jit(solution)/shard_map/all_gather | solution.py:92
  255.9 3.0 %convolution_convert_fusion = bf16[256,256]{1,0:T(8,128)(2,1)} fusion(bf16[4096,256]{1,0:T(8,128)(2,1)} %all-gather.5.cloned.1.call-done, bf16[4096,256]{1,0:T(8,128)(2,1)S(1)} %bitcast.88), kind=kOutput, calls=%fused_computation.9 | convolution fusion | flops 536936448 | bytes 4325376 | tf_op jit(solution)/shard_map/dot_general | solution.py:93
Async XLA Ops:
  6.5 128.2 %all-gather.3.cloned.1.call-start = ((), (), s32[]{:S(2)}) async-start(), calls=%async_computation.5 | async-start | bytes 6684672 | tf_op jit(solution)/shard_map/all_gather | solution.py:62
  10.9 15.3 %copy-start = (f32[2,256,512]{2,1,0:T(8,128)S(1)}, f32[2,256,512]{2,1,0:T(8,128)}, u32[]{:S(2)}) copy-start(f32[2,256,512]{2,1,0:T(8,128)} %param.7) | copy-start | bytes 3145732
  10.9 110.9 %all-to-all-start = ((bf16[16,256,256]{2,1,0:T(8,128)(2,1)}), bf16[16,256,256]{2,1,0:T(8,128)(2,1)S(1)}, u32[]{:S(2)}, u32[]{:S(2)}) async-start(bf16[16,256,256]{2,1,0:T(8,128)(2,1)} %broadcast_in_dim.4), calls=%async_computation | async-start | bytes 4194304 | tf_op jit(solution)/shard_map/all_to_all | solution.py:19
  121.9 23.2 %all-to-all-start.2 = ((f32[2,256,512]{2,0,1:T(2,128)}), f32[2,256,512]{2,0,1:T(2,128)S(1)}, u32[]{:S(2)}, u32[]{:S(2)}) async-start(f32[2,256,512]{2,0,1:T(2,128)} %copy.16), calls=%async_computation.2 | async-start | bytes 2097152 | tf_op jit(solution)/shard_map/all_to_all | solution.py:70
  139.4 0.9 copy-start.1
  145.1 12.6 %all-to-all-start.1 = ((f32[16,16,256]{2,1,0:T(8,128)}), f32[16,16,256]{2,1,0:T(8,128)S(1)}, u32[]{:S(2)}, u32[]{:S(2)}) async-start(f32[16,16,256]{2,1,0:T(8,128)} %bitcast.2), calls=%async_computation.1 | async-start | bytes 524288 | tf_op jit(solution)/shard_map/all_to_all | solution.py:71
  150.8 105.2 %all-gather.5.cloned.1.call-start = ((), (), s32[]{:S(2)}) async-start(), calls=%async_computation.6 | async-start | bytes 2228224 | tf_op jit(solution)/shard_map/all_gather | solution.py:92
  172.1 16.4 %copy-start.2 = (bf16[256,256]{1,0:T(8,128)(2,1)S(1)}, bf16[256,256]{1,0:T(8,128)(2,1)}, u32[]{:S(2)}) copy-start(bf16[256,256]{1,0:T(8,128)(2,1)} %param.6) | copy-start | bytes 393220
Sparse Core Ops, SparseCore 0:
  10.5 87.5 all-gather.2
  188.6 67.3 all-gather.4
where the time goes:
time: 266 us
  waiting for transfers between devices  134 us (50%)
  blocking collectives  45.1 us (17%)
  starting transfers between devices  28.5 us (11%)
  matrix products  22.8 us (9%)
  local copies, waits for them, and re-layouts  19 us (7%)
  between operations  13.6 us (5%)
  other arithmetic  2.67 us (1%)
    all_to_all x1, waiting for transfers between devices, copy_for_each(): lax.all_to_all(jnp.broadcast_to(array[None], (devices, *array.shape)), ax...  93.7 us
    all_gather x1, waiting for transfers between devices, body(): gathered = lax.all_gather(mixed, 'chan', axis=0, tiled=True)  35.7 us
    all_to_all x1, blocking collectives, copy_for_each(): lax.all_to_all(jnp.broadcast_to(array[None], (devices, *array.shape)), ax...  31.6 us
    all_to_all x1, starting transfers between devices, copy_for_each(): lax.all_to_all(jnp.broadcast_to(array[None], (devices, *array.shape)), ax...  15.3 us
    all_to_all x1, blocking collectives, body(): lax.all_to_all(signal, 'seq', split_axis=1, concat_axis=0, tiled=True)  13.5 us
    all_to_all x1, starting transfers between devices, body(): lax.all_to_all(spectrum, 'seq', split_axis=1, concat_axis=2, tiled=True)  7.45 us
    all_to_all x1, starting transfers between devices, body(): lax.all_to_all(mixed_in, 'seq', split_axis=0, concat_axis=1, tiled=True)  5.66 us
    reshape x2, local copies, waits for them, and re-layouts, body(): spread.reshape(2, sub_chan, tok_rows, twice_seq)  5.51 us
  transfers between devices with their start and end apart: 5, of which 4 were waited for; matrix products, arithmetic and copies ran while one was open for 8% of the time, Pallas kernels for 0%

commit v1 on v0

v1 whole, which is shorter than its diff:
```python
import functools
import math

import jax
import jax.numpy as jnp
import numpy as np
from jax import lax
from jax.experimental import pallas as pl
from jax.experimental.pallas import tpu as pltpu
from jax.sharding import PartitionSpec as P

MESH = pl.DeviceIdType.MESH
F32 = jnp.float32
BF16 = jnp.bfloat16


def tables():
    p = np.arange(256)[:, None]
    kappa = np.arange(512)[None, :]
    angle = 2.0 * math.pi * ((p * kappa) % 512) / 512.0
    first = np.concatenate([np.cos(angle), -np.sin(angle)], axis=1)
    m0 = np.arange(16)[:, None]
    s = np.arange(16)[None, :]
    turn = np.exp(-2j * math.pi * ((m0 * s) % 16) / 16.0)
    eye = np.eye(16)

    def blocks(table):
        wide = np.kron(table, eye)
        return np.block([[wide.real, -wide.imag], [wide.imag, wide.real]])

    twist = 2.0 * math.pi * m0 * kappa / 8192.0
    rows = np.arange(256)
    perm = np.zeros((256, 256))
    perm[rows, (rows % 16) * 16 + rows // 16] = 1.0
    return (
        jnp.asarray(first, BF16),
        jnp.asarray(blocks(turn), BF16),
        jnp.asarray(blocks(np.conj(turn)), BF16),
        jnp.asarray(np.stack([np.cos(twist), np.sin(twist)]), F32),
        jnp.asarray(perm, BF16),
    )


def swap_blocks(groups):
    lane = lax.broadcasted_iota(jnp.int32, (16, 256), 1) // 16
    for bit in range(4):
        step = 1 << bit
        low = (lane // step) % 2 == 0
        new = list(groups)
        for i in range(16):
            if i & step:
                continue
            j = i | step
            new[i] = jnp.where(low, groups[i], pltpu.roll(groups[j], 16 * step, 1))
            new[j] = jnp.where(low, pltpu.roll(groups[i], 256 - 16 * step, 1), groups[j])
        groups = new
    return groups


def kernel(
    tok, win, wout, spec, first_in, mix_in, unmix_in, twist_in, perm_in, out,
    tbuf, wbuf, obuf, mbuf, sraw, scast, sbuf, gbuf, xbuf, ybuf, rbuf, acc, total,
    first, mix, unmix, twist, perm,
    zt_send, zt_recv, zm_send, zm_recv, w_send, w_recv, o_send, o_recv,
    pair_send, pair_recv, many_send, many_recv, local,
):
    s = lax.axis_index("seq")
    z = lax.axis_index("chan")
    l = lax.axis_index("batch")
    x, h, core = s // 4, (s // 2) % 2, s % 2

    def at_seq(other):
        return {"seq": other}

    def seq_of(x_of, h_of):
        return (x_of % 4) * 4 + h_of * 2 + core

    sibling = at_seq(s + 1 - 2 * core)
    x_up, x_down = at_seq(seq_of(x + 1, h)), at_seq(seq_of(x + 3, h))
    y_same = {"batch": 1 - l}
    y_other = {"seq": seq_of(x, 1 - h), "batch": 1 - l}
    z_up, z_down = {"chan": (z + 1) % 16}, {"chan": (z + 15) % 16}
    sends = []

    barrier = pltpu.get_barrier_semaphore()
    for peer in [at_seq((s + j) % 16) for j in range(1, 16)] + [y_same, y_other, z_up, z_down]:
        pl.semaphore_signal(barrier, inc=1, device_id=peer, device_id_type=MESH)
    pl.semaphore_wait(barrier, 19)

    def remote(src, dst, send, recv, peer):
        return pltpu.make_async_remote_copy(
            src_ref=src, dst_ref=dst, send_sem=send, recv_sem=recv, device_id=peer, device_id_type=MESH
        )

    def ring_send(src, buf, sends_sem, recvs_sem, origin, way, d, p):
        dst = buf.at[origin, pl.ds(128 * p, 128)]
        copy = remote(dst if src is None else src, dst, sends_sem.at[way, d, p], recvs_sem.at[way, d, p],
                      z_up if way == 0 else z_down)
        copy.start()
        sends.append(copy)

    def ring_start(source, buf, sends_sem, recvs_sem):
        for p in range(2):
            for way in range(2):
                src = None if source is None else source.at[pl.ds(128 * p, 128)]
                ring_send(src, buf, sends_sem, recvs_sem, z, way, 0, p)

    def ring_step(buf, sends_sem, recvs_sem, d):
        for p in range(2):
            for way in range(2):
                if d == 8 and p != way:
                    continue
                origin = (z + 16 - d) % 16 if way == 0 else (z + d) % 16
                piece = buf.at[origin, pl.ds(128 * p, 128)]
                remote(piece, piece, sends_sem.at[way, d - 1, p], recvs_sem.at[way, d - 1, p], z_up).wait_recv()
                if d < 7 or (d == 7 and p == way):
                    ring_send(None, buf, sends_sem, recvs_sem, origin, way, d, p)

    def weight_events(source, buf, send, recv, pair):
        def piece(x_of, h_of, half):
            return buf.at[:, pl.ds(pl.multiple_of(seq_of(x_of, h_of) * 256 + half * 128, 128), 128)]

        def hand_on(ref, dst, at, peer):
            copy = remote(ref, dst, send.at[at], recv.at[at], peer)
            copy.start()
            sends.append(copy)

        def to_pair(ref, dst):
            remote(ref, dst, pair_send.at[pair], pair_recv.at[pair], sibling).start()

        def arrive(at, ref):
            remote(ref, ref, send.at[at], recv.at[at], sibling).wait_recv()
            to_pair(ref, ref)

        def start():
            own = lambda half: source.at[:, pl.ds(pl.multiple_of(half * 128, 128), 128)]
            hand_on(own(l), piece(x, h, l), 2, x_up)
            hand_on(own(l), piece(x, h, l), 3, x_down)
            hand_on(own(1 - l), piece(x, h, 1 - l), 0, y_other)
            hand_on(own(l), piece(x, h, l), 1, y_other)
            whole = buf.at[:, pl.ds(pl.multiple_of(s * 256, 256), 256)]
            to_pair(source, whole)
            pltpu.make_async_copy(source, whole, local.at[pair]).start()

        def first_y():
            ref = piece(x, 1 - h, l)
            arrive(0, ref)
            hand_on(ref, ref, 4, x_up)
            hand_on(ref, ref, 5, x_down)

        def first_x():
            ref = piece(x + 3, h, l)
            arrive(2, ref)
            hand_on(ref, ref, 6, x_up)
            hand_on(ref, ref, 8, y_same)
            hand_on(ref, ref, 12, y_other)
            ref = piece(x + 1, h, l)
            arrive(3, ref)
            hand_on(ref, ref, 9, y_same)
            hand_on(ref, ref, 13, y_other)

        def second_x():
            arrive(4, piece(x + 3, 1 - h, l))
            ref = piece(x + 1, 1 - h, l)
            arrive(5, ref)
            hand_on(ref, ref, 7, x_down)

        def second_y():
            arrive(1, piece(x, 1 - h, 1 - l))

        def third_x():
            ref = piece(x + 2, h, l)
            arrive(6, ref)
            hand_on(ref, ref, 10, y_same)
            ref = piece(x + 2, 1 - h, l)
            arrive(7, ref)
            hand_on(ref, ref, 11, y_same)

        def third_y():
            arrive(8, piece(x + 3, h, 1 - l))
            arrive(9, piece(x + 1, h, 1 - l))

        def fourth_y():
            arrive(12, piece(x + 3, 1 - h, 1 - l))
            arrive(13, piece(x + 1, 1 - h, 1 - l))

        def fifth_y():
            arrive(10, piece(x + 2, h, 1 - l))
            arrive(11, piece(x + 2, 1 - h, 1 - l))

        half_all = buf.at[:, pl.ds(0, 2048)]

        def finish():
            whole = buf.at[:, pl.ds(pl.multiple_of(s * 256, 256), 256)]
            pltpu.make_async_copy(source, whole, local.at[pair]).wait()
            remote(half_all, half_all, pair_send.at[pair], pair_recv.at[pair], sibling).wait_recv()

        def drain():
            remote(half_all, half_all, pair_send.at[pair], pair_recv.at[pair], sibling).wait_send()

        return (start, first_y, first_x, second_x, second_y, third_x, third_y, fourth_y, fifth_y, finish, drain)

    def spread(source, dest, at):
        for j in range(1, 16):
            peer = (s + j) % 16
            remote(source(peer), dest, many_send.at[at], many_recv.at[at], at_seq(peer)).start()

    def collect(ref, at):
        remote(ref, ref, many_send.at[at], many_recv.at[at], sibling).wait_recv()

    def drain_many(ref, at):
        remote(ref, ref, many_send.at[at], many_recv.at[at], sibling).wait_send()

    w = weight_events(win, wbuf, w_send, w_recv, 0)
    o = weight_events(wout, obuf, o_send, o_recv, 1)

    ring_start(tok, tbuf, zt_send, zt_recv)
    w[0]()
    own_tokens = pltpu.make_async_copy(tok, tbuf.at[z], local.at[2])
    own_tokens.start()
    raw = pltpu.make_async_copy(spec, sraw, local.at[3])
    raw.start()
    loads = [
        pltpu.make_async_copy(src, dst, local.at[4 + at])
        for at, (src, dst) in enumerate(
            ((first_in, first), (mix_in, mix), (unmix_in, unmix), (twist_in, twist), (perm_in, perm))
        )
    ]
    for load in loads:
        load.start()
    raw.wait()
    scast[...] = sraw[...].astype(BF16)

    def step_t(d):
        ring_step(tbuf, zt_send, zt_recv, d)

    step_t(1)
    w[1]()
    w[2]()
    step_t(2)

    def rows16(ref, at):
        return ref.at[:, pl.ds(pl.multiple_of(at * 16, 16), 16)]

    mine = rows16(sbuf, s)
    spread(lambda peer: rows16(scast, peer), mine, 0)
    own_rows = pl.ds(pl.multiple_of(s * 16, 16), 16)
    sbuf[:, own_rows, :] = scast[:, own_rows, :]
    step_t(3)
    w[3]()
    w[4]()
    step_t(4)
    w[5]()
    step_t(5)
    w[6]()
    step_t(6)
    w[7]()
    step_t(7)
    w[8]()
    own_tokens.wait()
    w[9]()

    acc[...] = jnp.zeros_like(acc)

    def project(origin):
        block = tbuf[origin]
        rows = pl.ds(pl.multiple_of(origin * 256, 256), 256)
        for j in range(3):
            acc[j] += jnp.dot(block, wbuf[j, rows, :], preferred_element_type=F32)

    project(z)
    for d in range(1, 8):
        project((z + 16 - d) % 16)
        project((z + d) % 16)
    step_t(8)
    project((z + 8) % 16)

    for load in loads:
        load.wait()
    gated = (acc[1] * acc[2]).astype(BF16)
    gated = jnp.dot(perm[...], gated, preferred_element_type=F32)
    groups = swap_blocks([gated[16 * i : 16 * i + 16, :] for i in range(16)])
    for i in range(16):
        gbuf[i] = groups[i].astype(BF16)
    spread(lambda peer: gbuf.at[peer], xbuf.at[s], 1)
    xbuf[s] = gbuf[s]
    collect(sbuf.at[:, pl.ds(0, 240)], 0)
    collect(xbuf.at[pl.ds(0, 15)], 1)

    signal = xbuf[...].reshape(256, 256).astype(F32).T.astype(BF16)
    spectrum = jnp.dot(signal, first[...], preferred_element_type=F32)
    a_re = spectrum[:, :512].reshape(16, 16, 512)
    a_im = spectrum[:, 512:].reshape(16, 16, 512)
    cos, sin = twist[0][:, None, :], twist[1][:, None, :]
    b_re = (a_re * cos + a_im * sin).reshape(256, 512)
    b_im = (a_im * cos - a_re * sin).reshape(256, 512)
    b = jnp.concatenate([b_re, b_im], axis=0).astype(BF16)
    u = jnp.dot(mix[...], b, preferred_element_type=F32)
    u_re, u_im = u[:256], u[256:]
    f_re, f_im = sbuf[0].astype(F32), sbuf[1].astype(F32)
    v = jnp.concatenate([u_re * f_re - u_im * f_im, u_re * f_im + u_im * f_re], axis=0).astype(BF16)
    c = jnp.dot(unmix[...], v, preferred_element_type=F32)
    c_re, c_im = c[:256].reshape(16, 16, 512), c[256:].reshape(16, 16, 512)
    d_re = (c_re * cos - c_im * sin).reshape(256, 512)
    d_im = (c_im * cos + c_re * sin).reshape(256, 512)
    d_all = jnp.concatenate([d_re, d_im], axis=1).astype(BF16)
    y = lax.dot_general(first[...], d_all, (((1,), (1,)), ((), ())), preferred_element_type=F32)
    ybuf[...] = (y * (1.0 / 8192.0)).astype(BF16).reshape(16, 16, 256)
    spread(lambda peer: ybuf.at[peer], rbuf.at[s], 2)
    rbuf[s] = ybuf[s]
    collect(rbuf.at[pl.ds(0, 15)], 2)

    groups = swap_blocks([rbuf[i].astype(F32) for i in range(16)])
    conv = jnp.concatenate(groups, axis=0).astype(BF16)
    conv = jnp.dot(perm[...], conv, preferred_element_type=F32)
    mbuf[z] = (acc[0] * conv).astype(BF16)

    ring_start(None, mbuf, zm_send, zm_recv)
    o[0]()
    total[...] = jnp.zeros_like(total)

    def step_m(d):
        ring_step(mbuf, zm_send, zm_recv, d)

    def combine(origin):
        rows = pl.ds(pl.multiple_of(origin * 256, 256), 256)
        total[...] += jnp.dot(mbuf[origin], obuf[0, rows, :], preferred_element_type=F32)

    step_m(1)
    o[1]()
    o[2]()
    step_m(2)
    o[3]()
    o[4]()
    o[5]()
    step_m(3)
    o[6]()
    o[7]()
    step_m(4)
    o[8]()
    o[9]()
    step_m(5)
    combine(z)
    for d in range(1, 8):
        if d > 5:
            step_m(d)
        combine((z + 16 - d) % 16)
        combine((z + d) % 16)
    step_m(8)
    combine((z + 8) % 16)
    out[...] = total[...].astype(BF16)

    for copy in sends:
        copy.wait_send()
    w[10]()
    o[10]()
    drain_many(sbuf.at[:, pl.ds(0, 240)], 0)
    drain_many(xbuf.at[pl.ds(0, 15)], 1)
    drain_many(rbuf.at[pl.ds(0, 15)], 2)


def body(tokens, in_weights, out_weights, spectrum):
    dma = pltpu.SemaphoreType.DMA
    any_spec = pl.BlockSpec(memory_space=pl.ANY)
    return pl.pallas_call(
        kernel,
        out_shape=jax.ShapeDtypeStruct((256, 256), BF16),
        in_specs=[any_spec] * 9,
        out_specs=pl.BlockSpec(memory_space=pltpu.VMEM),
        scratch_shapes=[
            pltpu.VMEM((16, 256, 256), BF16),
            pltpu.VMEM((3, 4096, 256), BF16),
            pltpu.VMEM((1, 4096, 256), BF16),
            pltpu.VMEM((16, 256, 256), BF16),
            pltpu.VMEM((2, 256, 512), F32),
            pltpu.VMEM((2, 256, 512), BF16),
            pltpu.VMEM((2, 256, 512), BF16),
            pltpu.VMEM((16, 16, 256), BF16),
            pltpu.VMEM((16, 16, 256), BF16),
            pltpu.VMEM((16, 16, 256), BF16),
            pltpu.VMEM((16, 16, 256), BF16),
            pltpu.VMEM((3, 256, 256), F32),
            pltpu.VMEM((256, 256), F32),
            pltpu.VMEM((256, 1024), BF16),
            pltpu.VMEM((512, 512), BF16),
            pltpu.VMEM((512, 512), BF16),
            pltpu.VMEM((2, 16, 512), F32),
            pltpu.VMEM((256, 256), BF16),
            dma((2, 8, 2)),
            dma((2, 8, 2)),
            dma((2, 8, 2)),
            dma((2, 8, 2)),
            dma((14,)),
            dma((14,)),
            dma((14,)),
            dma((14,)),
            dma((2,)),
            dma((2,)),
            dma((3,)),
            dma((3,)),
            dma((9,)),
        ],
        compiler_params=pltpu.CompilerParams(
            collective_id=0, has_side_effects=True, vmem_limit_bytes=48 * 1024 * 1024
        ),
    )(tokens, in_weights, out_weights[None], spectrum, *tables())


def solution(mesh):
    placed = (
        P(("batch", "seq"), "chan"),
        P(None, "seq", "chan"),
        P("seq", "chan"),
        P(None, "chan", "seq"),
    )
    return jax.shard_map(
        body, mesh=mesh, in_specs=placed, out_specs=P(("batch", "seq"), "chan"), check_vma=False
    )
```

time: 266 us -> 107 us (0.40)
  the two profiles are of different devices: /device:TPU:4 before, /device:TPU:2 now
where the time goes in v1:
time: 107 us
  Pallas kernels  97.1 us (91%)
  local copies, waits for them, and re-layouts  9.55 us (9%)
    pallas_call x1, Pallas kernels, body(): pl.pallas_call(kernel, out_shape=jax.ShapeDtypeStruct((256, 256), BF16),...  97.1 us
    unnamed x19, local copies, waits for them, and re-layouts  9.55 us

profile of v1, /device:TPU:2, one launch (start us, length us, event | category | flops | bytes accessed | tf_op | source)
XLA Modules:
  0.0 106.6 jit_solution(4496598694199718365)
XLA Ops:
  0.0 0.0 copy-start
  0.0 1.2 %copy-done = f32[2,256,512]{2,1,0:T(8,128)S(1)} copy-done((f32[2,256,512]{2,1,0:T(8,128)S(1)}, f32[2,256,512]{2,1,0:T(8,128)}, u32[]{:S(2)}) %copy-start) | copy-done | bytes 1048600
  1.2 0.0 copy-start.1
  1.2 1.0 copy-done.1
  2.3 0.0 copy-start.2
  2.3 1.0 copy-done.2
  3.3 0.0 copy-start.3
  3.3 1.0 copy-done.3
  4.4 0.0 copy-start.4
  4.4 1.0 copy-done.4
  5.3 0.0 copy-start.5
  5.4 0.9 copy-done.5
  6.3 0.0 copy-start.6
  6.3 0.9 copy-done.6
  7.2 0.0 copy-start.7
  7.2 0.9 copy-done.7
  8.1 0.0 copy-start.8
  8.1 0.8 copy-done.8
  8.9 97.1 %shard_map.91 = bf16[256,256]{1,0:T(8,128)(2,1)S(1)} custom-call(bf16[256,256]{1,0:T(8,128)(2,1)S(1)} %copy-done.5, bf16[3,256,256]{2,1,0:T(8,128)(2,1)S(1)} %copy-done.4, bf16[1,256,256]{2,1,0:T(8,128)(2,1)S(1)} %bitcast.1, f32[2,256,512]{2,1,0:T(8,128)S(1)} %copy-done, bf16[256,1024]{1,0:T(8,128)(2,1)S(1)} %copy-done.3, bf16[512,512]{1,0:T(8,128)(2,1)S(1)} %copy-done.2, ...), custom_call_target="tpu_custom_call" | custom-call | tf_op jit(solution)/shard_map/pallas_call | solution.py:365
  106.0 0.7 copy.11
Async XLA Ops:
  0.0 1.2 %copy-start = (f32[2,256,512]{2,1,0:T(8,128)S(1)}, f32[2,256,512]{2,1,0:T(8,128)}, u32[]{:S(2)}) copy-start(f32[2,256,512]{2,1,0:T(8,128)} %spec.1) | copy-start | bytes 3145732
  1.2 1.0 copy-start.1
  2.3 1.0 copy-start.2
  3.3 1.0 copy-start.3
  4.4 1.0 copy-start.4
  5.3 0.9 copy-start.5
  6.3 0.9 copy-start.6
  7.2 0.9 copy-start.7
  8.1 0.8 copy-start.8

commit v2 on v1

v2 whole, which is shorter than its diff:
```python
import math

import jax
import jax.numpy as jnp
import numpy as np
from jax import lax
from jax.experimental import pallas as pl
from jax.experimental.pallas import tpu as pltpu
from jax.sharding import PartitionSpec as P

MESH = pl.DeviceIdType.MESH
F32 = jnp.float32
BF16 = jnp.bfloat16


def tables():
    p = np.arange(256)[:, None]
    kappa = np.arange(512)[None, :]
    angle = 2.0 * math.pi * ((p * kappa) % 512) / 512.0
    m0 = np.arange(16)[:, None]
    s = np.arange(16)[None, :]
    turn = np.exp(-2j * math.pi * ((m0 * s) % 16) / 16.0)

    def blocks(table):
        wide = np.kron(table, np.eye(8))
        return np.block([[wide.real, -wide.imag], [wide.imag, wide.real]])

    twist = 2.0 * math.pi * m0 * kappa / 8192.0
    rows = np.arange(256)
    by_m0 = np.eye(256)[(rows % 16) * 16 + rows // 16]
    by_owner = np.eye(256)[(rows // 8 % 2) * 128 + rows // 16 * 8 + rows % 8]
    wide = [np.cos(angle), -np.sin(angle), blocks(turn), blocks(np.conj(turn)), by_m0, by_owner]
    return (
        jnp.asarray(np.concatenate(wide, axis=1), BF16),
        jnp.asarray(np.stack([np.cos(twist), np.sin(twist)]), F32),
    )


def swap_blocks(groups):
    lane = lax.broadcasted_iota(jnp.int32, (16, 128), 1) // 8
    for bit in range(4):
        step = 1 << bit
        low = (lane // step) % 2 == 0
        new = list(groups)
        for i in range(16):
            if i & step:
                continue
            j = i | step
            new[i] = jnp.where(low, groups[i], pltpu.roll(groups[j], 8 * step, 1))
            new[j] = jnp.where(low, pltpu.roll(groups[i], 128 - 8 * step, 1), groups[j])
        groups = new
    return groups


def kernel(
    tok, win, wout, spec, table_in, twist_in, out,
    tbuf, wbuf, obuf, mbuf, sraw, scast, sbuf, gbuf, xbuf, ybuf, rbuf, acc, total, table, twist,
    zt_send, zt_recv, zm_send, zm_recv, w_send, w_recv, pair_send, pair_recv, many_send, many_recv, local,
):
    s = lax.axis_index("seq")
    z = lax.axis_index("chan")
    l = lax.axis_index("batch")
    x, h, core = s // 4, (s // 2) % 2, s % 2

    def at_seq(other):
        return {"seq": other}

    def seq_of(x_of, h_of):
        return (x_of % 4) * 4 + h_of * 2 + core

    sibling = at_seq(s + 1 - 2 * core)
    x_up, x_down = at_seq(seq_of(x + 1, h)), at_seq(seq_of(x + 3, h))
    y_same = {"batch": 1 - l}
    y_other = {"seq": seq_of(x, 1 - h), "batch": 1 - l}
    z_at = lambda step: {"chan": (z + 16 + step) % 16}
    sends = []

    barrier = pltpu.get_barrier_semaphore()
    peers = [at_seq((s + j) % 16) for j in range(1, 16)] + [y_same, y_other] + [z_at(step) for step in (1, -1, 2, -2)]
    for peer in peers:
        pl.semaphore_signal(barrier, inc=1, device_id=peer, device_id_type=MESH)
    raw = pltpu.make_async_copy(spec, sraw, local.at[8])
    loads = [
        pltpu.make_async_copy(table_in, table, local.at[9]),
        pltpu.make_async_copy(twist_in, twist, local.at[10]),
    ]
    for load in [raw] + loads:
        load.start()
    pl.semaphore_wait(barrier, len(peers))

    def remote(src, dst, send, recv, peer):
        return pltpu.make_async_remote_copy(
            src_ref=src, dst_ref=dst, send_sem=send, recv_sem=recv, device_id=peer, device_id_type=MESH
        )

    def ring(source, buf, sends_sem, recvs_sem):
        def send(origin, way, d, p, step):
            dst = buf.at[origin, p]
            src = source.at[pl.ds(64 * p, 64)] if d == 1 and source is not None else dst
            peer = z_at(step if way == 0 else -step)
            copy = remote(src, dst, sends_sem.at[way, d - 1, p], recvs_sem.at[way, d - 1, p], peer)
            copy.start()
            sends.append(copy)

        def start(pieces):
            for p in pieces:
                for way in range(2):
                    send(z, way, 1, p, 1)

        def take(d, p):
            for way in range(2):
                if d == 8 and p % 2 != way:
                    continue
                origin = (z + 16 - d) % 16 if way == 0 else (z + d) % 16
                piece = buf.at[origin, p]
                remote(piece, piece, sends_sem.at[way, d - 1, p], recvs_sem.at[way, d - 1, p], z_at(1)).wait_recv()
                if d < 7:
                    send(origin, way, d + 1, p, 1)
                if d == 6 and p % 2 == way:
                    send(origin, way, 8, p, 2)

        return start, take

    def weight_events(source, buf, pair):
        def piece(x_of, h_of, half):
            return buf.at[pl.ds(pl.multiple_of(seq_of(x_of, h_of) * 256 + half * 128, 128), 128)]

        def hand_on(ref, dst, at, peer):
            copy = remote(ref, dst, w_send.at[pair, at], w_recv.at[pair, at], peer)
            copy.start()
            sends.append(copy)

        def to_pair(ref, dst):
            remote(ref, dst, pair_send.at[pair], pair_recv.at[pair], sibling).start()

        def arrive(at, ref):
            remote(ref, ref, w_send.at[pair, at], w_recv.at[pair, at], sibling).wait_recv()
            to_pair(ref, ref)

        def start():
            own = lambda half: source.at[pl.ds(pl.multiple_of(half * 128, 128), 128)]
            hand_on(own(l), piece(x, h, l), 2, x_up)
            hand_on(own(l), piece(x, h, l), 3, x_down)
            hand_on(own(1 - l), piece(x, h, 1 - l), 0, y_other)
            hand_on(own(l), piece(x, h, l), 1, y_other)
            whole = buf.at[pl.ds(pl.multiple_of(s * 256, 256), 256)]
            to_pair(source, whole)
            pltpu.make_async_copy(source, whole, local.at[pair]).start()

        def y1():
            ref = piece(x, 1 - h, l)
            arrive(0, ref)
            hand_on(ref, ref, 4, x_up)
            hand_on(ref, ref, 5, x_down)

        def x1():
            ref = piece(x + 3, h, l)
            arrive(2, ref)
            hand_on(ref, ref, 6, x_up)
            hand_on(ref, ref, 8, y_same)
            hand_on(ref, ref, 12, y_other)
            ref = piece(x + 1, h, l)
            arrive(3, ref)
            hand_on(ref, ref, 9, y_same)
            hand_on(ref, ref, 13, y_other)

        def y2():
            arrive(1, piece(x, 1 - h, 1 - l))

        def x2():
            ref = piece(x + 1, 1 - h, l)
            arrive(5, ref)
            hand_on(ref, ref, 7, x_down)

        def x3():
            arrive(4, piece(x + 3, 1 - h, l))

        def x4():
            ref = piece(x + 2, h, l)
            arrive(6, ref)
            hand_on(ref, ref, 10, y_same)

        def x5():
            ref = piece(x + 2, 1 - h, l)
            arrive(7, ref)
            hand_on(ref, ref, 11, y_same)

        def y3():
            arrive(8, piece(x + 3, h, 1 - l))
            arrive(9, piece(x + 1, h, 1 - l))

        def y4():
            arrive(12, piece(x + 3, 1 - h, 1 - l))
            arrive(13, piece(x + 1, 1 - h, 1 - l))

        def y5():
            arrive(10, piece(x + 2, h, 1 - l))
            arrive(11, piece(x + 2, 1 - h, 1 - l))

        half_all = buf.at[pl.ds(0, 2048)]

        def finish():
            whole = buf.at[pl.ds(pl.multiple_of(s * 256, 256), 256)]
            pltpu.make_async_copy(source, whole, local.at[pair]).wait()
            remote(half_all, half_all, pair_send.at[pair], pair_recv.at[pair], sibling).wait_recv()

        def drain():
            remote(half_all, half_all, pair_send.at[pair], pair_recv.at[pair], sibling).wait_send()

        steps = (start, y1, x1, y2, x2, x3, x4, x5, y3, y4, y5, finish, drain)
        return {step.__name__: step for step in steps}

    def spread(source, dest, at):
        for j in range(1, 16):
            peer = (s + j) % 16
            remote(source(peer), dest, many_send.at[at], many_recv.at[at], at_seq(peer)).start()

    def collect(ref, at):
        remote(ref, ref, many_send.at[at], many_recv.at[at], sibling).wait_recv()

    def drain_many(ref, at):
        remote(ref, ref, many_send.at[at], many_recv.at[at], sibling).wait_send()

    w = [weight_events(win.at[j], wbuf.at[j], j) for j in range(3)]
    o = weight_events(wout, obuf, 3)

    start_t, take_t = ring(tok, tbuf, zt_send, zt_recv)
    start_m, take_m = ring(None, mbuf, zm_send, zm_recv)

    start_t(range(4))
    for j in (1, 2, 0):
        w[j]["start"]()
    own_tokens = [
        pltpu.make_async_copy(tok.at[pl.ds(64 * p, 64)], tbuf.at[z, p], local.at[4 + p]) for p in range(4)
    ]
    for load in own_tokens:
        load.start()
    raw.wait()
    for load in loads:
        load.wait()
    for part in range(2):
        rows = jnp.dot(table[:, 1792:], sraw[part].astype(BF16), preferred_element_type=F32)
        scast[part] = rows.astype(BF16)

    def rows16(ref, at):
        return ref.at[:, pl.ds(pl.multiple_of(at * 16, 16), 16)]

    def spread_spectrum():
        spread(lambda peer: rows16(scast, peer), rows16(sbuf, s), 0)
        own_rows = pl.ds(pl.multiple_of(s * 16, 16), 16)
        sbuf[:, own_rows, :] = scast[:, own_rows, :]

    plan = {
        (1, 2): "1y1 1x1",
        (1, 3): "2y1 2x1",
        (2, 1): "0y1 0x1",
        (2, 3): "1y2 1x2",
        (3, 0): "2y2 1x3",
        (3, 1): "1x4 1y3",
        (3, 2): "2x2 0y2",
        (3, 3): "0x2 2x3",
        (4, 0): "1x5 2y3",
        (4, 1): "2x4 1y4",
        (4, 2): "0x3",
        (4, 3): "2x5",
        (5, 0): "0x4 0x5 0y3",
        (5, 1): "2y4",
        (6, 0): "0y4 1y5",
        (6, 3): "2y5",
        (7, 2): "0y5",
    }
    for d in range(1, 8):
        for p in range(4):
            take_t(d, p)
            for word in plan.get((d, p), "").split():
                w[int(word[0])][word[1:]]()
            if (d, p) == (5, 2):
                spread_spectrum()
    for load in own_tokens:
        load.wait()
    w[1]["finish"]()
    w[2]["finish"]()

    def project(origin, which, fresh=False):
        block = tbuf[origin].reshape(256, 256)
        rows = pl.ds(pl.multiple_of(origin * 256, 256), 256)
        for j in which:
            part = jnp.dot(block, wbuf[j, rows, :], preferred_element_type=F32)
            acc[j] = part if fresh else acc[j] + part

    def project_near(which):
        project(z, which, True)
        for d in range(1, 8):
            project((z + 16 - d) % 16, which)
            project((z + d) % 16, which)

    project_near((1, 2))
    for p in range(4):
        take_t(8, p)
    project((z + 8) % 16, (1, 2))

    by_m0 = table[:, 1536:1792]
    for half in range(2):
        lanes = slice(128 * half, 128 * half + 128)
        gated = (acc[1, :, lanes] * acc[2, :, lanes]).astype(BF16)
        gated = jnp.dot(by_m0, gated, preferred_element_type=F32)
        groups = swap_blocks([gated[16 * i : 16 * i + 16, :] for i in range(16)])
        for i in range(16):
            gbuf[half, i] = groups[i].astype(BF16)
        spread(lambda peer: gbuf.at[half, peer], xbuf.at[half, s], 1 + half)
        xbuf[half, s] = gbuf[half, s]

    w[0]["finish"]()
    project_near((0,))
    project((z + 8) % 16, (0,))
    collect(sbuf.at[:, pl.ds(0, 240)], 0)

    cos, sin = twist[0][:, None, :], twist[1][:, None, :]
    first, mix, unmix = table[:, :1024], table[:, 1024:1280], table[:, 1280:1536]
    for half in range(2):
        collect(xbuf.at[half, pl.ds(0, 15)], 1 + half)
        signal = xbuf[half].reshape(256, 128).astype(F32).T.astype(BF16)
        a = jnp.dot(signal, first, preferred_element_type=F32)
        a_re, a_im = a[:, :512].reshape(16, 8, 512), a[:, 512:].reshape(16, 8, 512)
        b_re = (a_re * cos + a_im * sin).reshape(128, 512)
        b_im = (a_im * cos - a_re * sin).reshape(128, 512)
        b = jnp.concatenate([b_re, b_im], axis=0).astype(BF16)
        u = jnp.dot(mix, b, preferred_element_type=F32)
        u_re, u_im = u[:128], u[128:]
        f_re, f_im = (
            sbuf[part].astype(F32).reshape(16, 2, 8, 512)[:, half].reshape(128, 512) for part in range(2)
        )
        v = jnp.concatenate([u_re * f_re - u_im * f_im, u_re * f_im + u_im * f_re], axis=0).astype(BF16)
        c = jnp.dot(unmix, v, preferred_element_type=F32)
        c_re, c_im = c[:128].reshape(16, 8, 512), c[128:].reshape(16, 8, 512)
        d_re = (c_re * cos - c_im * sin).reshape(128, 512)
        d_im = (c_im * cos + c_re * sin).reshape(128, 512)
        d_all = jnp.concatenate([d_re, d_im], axis=1).astype(BF16)
        y = lax.dot_general(first, d_all, (((1,), (1,)), ((), ())), preferred_element_type=F32)
        ybuf[half] = (y * (1.0 / 8192.0)).astype(BF16).reshape(16, 16, 128)
        spread(lambda peer: ybuf.at[half, peer], rbuf.at[half, s], 3 + half)
        rbuf[half, s] = ybuf[half, s]

    for half in range(2):
        collect(rbuf.at[half, pl.ds(0, 15)], 3 + half)
        groups = swap_blocks([rbuf[half, i].astype(F32) for i in range(16)])
        conv = jnp.concatenate(groups, axis=0).astype(BF16)
        conv = jnp.dot(by_m0, conv, preferred_element_type=F32)
        mixed = (acc[0, :, 128 * half : 128 * half + 128] * conv).astype(BF16)
        mbuf[z, 2 * half] = mixed[:128]
        mbuf[z, 2 * half + 1] = mixed[128:]
        start_m((2 * half, 2 * half + 1))

    o["start"]()
    total[...] = jnp.zeros_like(total)

    def combine(origin):
        for half in range(2):
            rows = pl.ds(pl.multiple_of(origin * 256 + 128 * half, 128), 128)
            block = jnp.concatenate([mbuf[origin, 2 * half], mbuf[origin, 2 * half + 1]], axis=0)
            total[...] += jnp.dot(block, obuf[rows, :], preferred_element_type=F32)

    plan = {
        (1, 2): "y1 x1",
        (2, 0): "y2",
        (2, 3): "x2 x3",
        (3, 1): "x4 y3 y4",
        (4, 0): "x5",
        (5, 1): "y5",
        (5, 3): "finish",
    }
    for d in range(1, 8):
        for p in range(4):
            take_m(d, p)
            for word in plan.get((d, p), "").split():
                o[word]()
        if d == 6:
            combine(z)
            for near in range(1, 4):
                combine((z + 16 - near) % 16)
                combine((z + near) % 16)
    for near in range(4, 8):
        combine((z + 16 - near) % 16)
        combine((z + near) % 16)
    for p in range(4):
        take_m(8, p)
    combine((z + 8) % 16)
    out[...] = total[...].astype(BF16)

    for copy in sends:
        copy.wait_send()
    for each in w + [o]:
        each["drain"]()
    drain_many(sbuf.at[:, pl.ds(0, 240)], 0)
    for half in range(2):
        drain_many(xbuf.at[half, pl.ds(0, 15)], 1 + half)
        drain_many(rbuf.at[half, pl.ds(0, 15)], 3 + half)


def body(tokens, in_weights, out_weights, spectrum):
    dma = pltpu.SemaphoreType.DMA
    any_spec = pl.BlockSpec(memory_space=pl.ANY)
    return pl.pallas_call(
        kernel,
        out_shape=jax.ShapeDtypeStruct((256, 256), BF16),
        in_specs=[any_spec] * 6,
        out_specs=pl.BlockSpec(memory_space=pltpu.VMEM),
        scratch_shapes=[
            pltpu.VMEM((16, 4, 64, 256), BF16),
            pltpu.VMEM((3, 4096, 256), BF16),
            pltpu.VMEM((4096, 256), BF16),
            pltpu.VMEM((16, 4, 128, 128), BF16),
            pltpu.VMEM((2, 256, 512), F32),
            pltpu.VMEM((2, 256, 512), BF16),
            pltpu.VMEM((2, 256, 512), BF16),
            pltpu.VMEM((2, 16, 16, 128), BF16),
            pltpu.VMEM((2, 16, 16, 128), BF16),
            pltpu.VMEM((2, 16, 16, 128), BF16),
            pltpu.VMEM((2, 16, 16, 128), BF16),
            pltpu.VMEM((3, 256, 256), F32),
            pltpu.VMEM((256, 256), F32),
            pltpu.VMEM((256, 2048), BF16),
            pltpu.VMEM((2, 16, 512), F32),
            dma((2, 8, 4)),
            dma((2, 8, 4)),
            dma((2, 8, 4)),
            dma((2, 8, 4)),
            dma((4, 14)),
            dma((4, 14)),
            dma((4,)),
            dma((4,)),
            dma((5,)),
            dma((5,)),
            dma((11,)),
        ],
        compiler_params=pltpu.CompilerParams(
            collective_id=0, has_side_effects=True, vmem_limit_bytes=60 * 1024 * 1024
        ),
    )(tokens, in_weights, out_weights, spectrum, *tables())


def solution(mesh):
    placed = (
        P(("batch", "seq"), "chan"),
        P(None, "seq", "chan"),
        P("seq", "chan"),
        P(None, "chan", "seq"),
    )
    return jax.shard_map(
        body, mesh=mesh, in_specs=placed, out_specs=P(("batch", "seq"), "chan"), check_vma=False
    )
```

time: 107 us -> 91.6 us (0.86)
  the two profiles are of different devices: /device:TPU:2 before, /device:TPU:1 now
where the time goes in v2:
time: 91.6 us; the launch traced here: 91.4 us
  Pallas kernels  89.9 us (98%)
  local copies, waits for them, and re-layouts  1.57 us (2%)
    pallas_call x1, Pallas kernels, body(): pl.pallas_call(kernel, out_shape=jax.ShapeDtypeStruct((256, 256), BF16),...  89.9 us

profile of v2, /device:TPU:1, one launch (start us, length us, event | category | flops | bytes accessed | tf_op | source)
XLA Modules:
  0.0 91.4 jit_solution(2063054386777186851)
XLA Ops:
  0.0 89.9 %shard_map.64 = bf16[256,256]{1,0:T(8,128)(2,1)} custom-call(bf16[256,256]{1,0:T(8,128)(2,1)} %tok.1, bf16[3,256,256]{2,1,0:T(8,128)(2,1)} %win.1, bf16[256,256]{1,0:T(8,128)(2,1)} %wout.1, f32[2,256,512]{2,1,0:T(8,128)} %spec.1, bf16[256,2048]{1,0:T(8,128)(2,1)} %constant.4.clone.table_in, f32[2,16,512]{2,1,0:T(8,128)} %constant.5.clone.twist_in), custom_call_target="tpu_custom_call" | custom-call | tf_op jit(solution)/shard_map/pallas_call | solution.py:403
  89.9 1.6 %copy.8 = bf16[256,256]{1,0:T(8,128)(2,1)} copy(bf16[256,256]{1,0:T(8,128)(2,1)} %shard_map.64) | data formatting | bytes 262144

commit v3 on v2

--- a/solution.py
+++ b/solution.py
@@ -267,7 +267,7 @@
         (5, 1): "2y4",
         (6, 0): "0y4 1y5",
         (6, 3): "2y5",
-        (7, 2): "0y5",
+        (7, 0): "0y5",
     }
     for d in range(1, 8):
         for p in range(4):
@@ -310,6 +310,7 @@
         spread(lambda peer: gbuf.at[half, peer], xbuf.at[half, s], 1 + half)
         xbuf[half, s] = gbuf[half, s]
 
+    o["start"]()
     w[0]["finish"]()
     project_near((0,))
     project((z + 8) % 16, (0,))
@@ -340,6 +341,9 @@
         ybuf[half] = (y * (1.0 / 8192.0)).astype(BF16).reshape(16, 16, 128)
         spread(lambda peer: ybuf.at[half, peer], rbuf.at[half, s], 3 + half)
         rbuf[half, s] = ybuf[half, s]
+    o["y1"]()
+    o["x1"]()
+    o["y2"]()
 
     for half in range(2):
         collect(rbuf.at[half, pl.ds(0, 15)], 3 + half)
@@ -351,40 +355,31 @@
         mbuf[z, 2 * half + 1] = mixed[128:]
         start_m((2 * half, 2 * half + 1))
 
-    o["start"]()
     total[...] = jnp.zeros_like(total)
 
     def combine(origin):
-        for half in range(2):
-            rows = pl.ds(pl.multiple_of(origin * 256 + 128 * half, 128), 128)
-            block = jnp.concatenate([mbuf[origin, 2 * half], mbuf[origin, 2 * half + 1]], axis=0)
-            total[...] += jnp.dot(block, obuf[rows, :], preferred_element_type=F32)
+        rows = pl.ds(pl.multiple_of(origin * 256, 256), 256)
+        halves = [jnp.concatenate([mbuf[origin, 2 * half], mbuf[origin, 2 * half + 1]], axis=0) for half in range(2)]
+        block = jnp.concatenate(halves, axis=1)
+        total[...] += jnp.dot(block, obuf[rows, :], preferred_element_type=F32)
 
     plan = {
-        (1, 2): "y1 x1",
-        (2, 0): "y2",
-        (2, 3): "x2 x3",
-        (3, 1): "x4 y3 y4",
-        (4, 0): "x5",
-        (5, 1): "y5",
-        (5, 3): "finish",
+        (1, 0): "x2 x3",
+        (1, 2): "y3 y4 x4",
+        (2, 1): "x5",
+        (3, 0): "y5",
+        (4, 0): "finish",
     }
-    for d in range(1, 8):
+    ready = [[], [], [], [], [0, 1, 2], [3, 4], [5, 6], [7], [8]]
+    for d in range(1, 9):
         for p in range(4):
             take_m(d, p)
             for word in plan.get((d, p), "").split():
                 o[word]()
-        if d == 6:
-            combine(z)
-            for near in range(1, 4):
-                combine((z + 16 - near) % 16)
+        for near in ready[d]:
+            combine((z + 16 - near) % 16)
+            if 0 < near < 8:
                 combine((z + near) % 16)
-    for near in range(4, 8):
-        combine((z + 16 - near) % 16)
-        combine((z + near) % 16)
-    for p in range(4):
-        take_m(8, p)
-    combine((z + 8) % 16)
     out[...] = total[...].astype(BF16)
 
     for copy in sends:

time: 91.6 us -> 88.8 us (0.969)
  the two profiles are of different devices: /device:TPU:1 before, /device:TPU:8 now
where the time goes in v3:
time: 88.8 us; the launch traced here: 88.7 us
  Pallas kernels  87.1 us (98%)
  local copies, waits for them, and re-layouts  1.57 us (2%)
    pallas_call x1, Pallas kernels, body(): pl.pallas_call(kernel, out_shape=jax.ShapeDtypeStruct((256, 256), BF16),...  87.1 us

profile of v3, /device:TPU:8, one launch (start us, length us, event | category | flops | bytes accessed | tf_op | source)
XLA Modules:
  0.0 88.7 jit_solution(1053741688741417134)
XLA Ops:
  0.0 87.1 %shard_map.64 = bf16[256,256]{1,0:T(8,128)(2,1)} custom-call(bf16[256,256]{1,0:T(8,128)(2,1)} %tok.1, bf16[3,256,256]{2,1,0:T(8,128)(2,1)} %win.1, bf16[256,256]{1,0:T(8,128)(2,1)} %wout.1, f32[2,256,512]{2,1,0:T(8,128)} %spec.1, bf16[256,2048]{1,0:T(8,128)(2,1)} %constant.4.clone.table_in, f32[2,16,512]{2,1,0:T(8,128)} %constant.5.clone.twist_in), custom_call_target="tpu_custom_call" | custom-call | tf_op jit(solution)/shard_map/pallas_call | solution.py:398
  87.1 1.6 %copy.8 = bf16[256,256]{1,0:T(8,128)(2,1)} copy(bf16[256,256]{1,0:T(8,128)(2,1)} %shard_map.64) | data formatting | bytes 262144
